TPU v7x, 128 devices: a whole 4x4x4 slice. The times are simulated.
128 devices in a mesh: fsdp: 16 (over x, z_hi, core), tp: 8 (over z_lo, y).
Axes of the slice: x: 4, y: 4, z: 4 (z_hi: 2, z_lo: 2; z = z_hi * 2 + z_lo), core: 2. Of those that a mesh axis runs over, the one named last changes fastest.
Arguments:
- activations: bfloat16 [8192, 5120], P('fsdp'), may hold values from -80 to 80
- cotangent: bfloat16 [8192, 5120], P('fsdp'), may hold values from -80 to 80
- lengths: int32 [32], P('fsdp'), may hold values from 64 to 256, as said below
- grow_operator: bfloat16 [5120, 4096], P('fsdp', 'tp'), may hold values from -0.078125 to 0.078125
- proxy_weight: bfloat16 [4096, 4096], P('fsdp', 'tp'), may hold values from -0.09375 to 0.09375
Outputs:
- update: bfloat16 [5120, 4096], P('fsdp', 'tp')
Inputs may be any that keep to these rules, and one draw needn't show every extreme that they name: `lengths`: each entry is the length of one sequence; at least one is 256 and at least one is 64.
All inputs are finite; a program needn't handle non-finite values.
Results may differ from a plain program's by a relative error of at most 0.0057.
Values may be sent and summed in bfloat16 or wider, within the bound.
A program may use at most 128 MiB of HBM per device.

v0:
```python
import jax
import jax.numpy as jnp
from jax import lax
from jax.sharding import PartitionSpec as P

D = 5120
PD = 4096
LEN = 256


def contract_tokens(left, right):
    return lax.dot_general(
        left, right, (((0,), (0,)), ((), ())), preferred_element_type=jnp.float32
    )


def contract_last(left, right):
    return lax.dot_general(
        left, right, (((1,), (1,)), ((), ())), preferred_element_type=jnp.float32
    )


def per_device(activations, cotangent, lengths, grow_operator, proxy_weight):
    keep_mask = (jnp.arange(LEN, dtype=jnp.int32)[None, :] < lengths[:, None]).reshape(-1)
    grad_rows = jnp.where(keep_mask[:, None], cotangent, jnp.zeros_like(cotangent))
    operator_cols, proxy_cols = (
        lax.all_gather(grow_operator, "fsdp", axis=0, tiled=True),
        lax.all_gather(proxy_weight, "fsdp", axis=0, tiled=True),
    )
    forward_cols = jnp.dot(activations, operator_cols, preferred_element_type=jnp.float32).astype(
        jnp.bfloat16
    )
    back_cols = jnp.dot(grad_rows, operator_cols, preferred_element_type=jnp.float32).astype(
        jnp.bfloat16
    )
    summed = lax.psum_scatter(
        contract_last(forward_cols, proxy_cols), "tp", scatter_dimension=1, tiled=True
    )
    proxy_out = summed.astype(jnp.bfloat16)
    back_all = lax.all_gather(back_cols, "tp", axis=1, tiled=True)
    delta_cols = jnp.dot(back_all, proxy_cols, preferred_element_type=jnp.float32).astype(
        jnp.bfloat16
    )
    grad_block = lax.psum_scatter(
        contract_tokens(activations, delta_cols) + contract_tokens(grad_rows, proxy_out),
        "fsdp",
        scatter_dimension=0,
        tiled=True,
    )
    total = lax.psum(jnp.sum(grad_block * grad_block), ("fsdp", "tp"))
    mean_sq = total / (D * PD)
    return (grad_block * lax.rsqrt(mean_sq + 1e-06)).astype(jnp.bfloat16)


def solution(mesh):
    placed = (P("fsdp", None), P("fsdp", None), P("fsdp"), P("fsdp", "tp"), P("fsdp", "tp"))
    return jax.shard_map(
        per_device, mesh=mesh, in_specs=placed, out_specs=P("fsdp", "tp"), check_vma=False
    )
```

profile of v0, /device:TPU:0, one launch (start us, length us, event | category | flops | bytes accessed | tf_op | source)
XLA Modules:
  0.0 502.7 jit_solution(2183676582384357263)
XLA Ops:
  6.5 0.7 all-gather.8.cloned.1.call-update
  7.3 0.0 all-gather.4.cloned.1.call-start
  7.3 0.7 all-gather.4.cloned.1.call-update
  8.0 0.0 reduce-scatter.5.cloned.1.call-start
  8.1 60.2 %all-gather.8.cloned.1.call-done = bf16[4096,512]{1,0:T(8,128)(2,1)} async-done(((bf16[256,512]{1,0:T(8,128)(2,1)}), bf16[4096,512]{1,0:T(8,128)(2,1)}) %all-gather.8.cloned.1.call-update) | async-done | bytes 4194320 | tf_op jit(solution)/shard_map/all_gather | solution.py:28
  68.3 61.0 %all-gather.4.cloned.1.call-done = bf16[5120,512]{1,0:T(8,128)(2,1)} async-done(((bf16[320,512]{1,0:T(8,128)(2,1)}), bf16[5120,512]{1,0:T(8,128)(2,1)}) %all-gather.4.cloned.1.call-update) | async-done | bytes 5242896 | tf_op jit(solution)/shard_map/all_gather | solution.py:27
  129.3 13.5 %fusion.3 = f32[512,4096]{1,0:T(8,128)} fusion(bf16[4096,512]{1,0:T(8,128)(2,1)} %all-gather.8.cloned.1.call-done, bf16[512,5120]{1,0:T(8,128)(2,1)} %param.5, bf16[5120,512]{1,0:T(8,128)(2,1)} %all-gather.4.cloned.1.call-done), kind=kOutput, calls=%fused_computation.8 | convolution fusion | flops 4832100352 | bytes 23068672 | tf_op jit(solution)/shard_map/dot_general | solution.py:18
  142.8 0.0 reduce-scatter.5.cloned.1.call-update
  142.8 0.0 all-gather.6.cloned.1.call-start
  142.9 0.6 copy-done
  143.5 0.1 iota_compare_fusion
  143.6 7.8 %fusion.2 = bf16[512,512]{1,0:T(8,128)(2,1)} fusion(bf16[5120,512]{1,0:T(8,128)(2,1)} %all-gather.4.cloned.1.call-done, bf16[512,5120]{1,0:T(8,128)(2,1)} %param.6, pred[512]{0:T(512)(128)(4,1)S(1)} %lt.23), kind=kOutput, calls=%fused_computation.4 | convolution fusion | flops 2687238144 | bytes 11010560 | tf_op jit(solution)/shard_map/dot_general | solution.py:33
  151.3 0.0 all-gather.6.cloned.1.call-update
  151.4 0.2 reduce-scatter.7.cloned.1.call-start
  151.6 82.8 %reduce-scatter.5.cloned.1.call-done = f32[512,512]{1,0:T(8,128)} async-done(((f32[512,4096]{1,0:T(8,128)}), f32[512,512]{1,0:T(8,128)}) %reduce-scatter.5.cloned.1.call-update) | async-done | bytes 1048592 | tf_op jit(solution)/shard_map/reduce_scatter | solution.py:36
  234.4 9.7 %fusion = f32[5120,512]{0,1:T(8,128)} fusion(bf16[512,5120]{1,0:T(8,128)(2,1)} %param.6, pred[512]{0:T(512)(128)(4,1)S(1)} %lt.23, f32[512,512]{1,0:T(8,128)} %reduce-scatter.5.cloned.1.call-done), kind=kOutput, calls=%fused_computation.2 | convolution fusion | flops 2687238144 | bytes 16777728 | tf_op jit(solution)/shard_map/dot_general | solution.py:12
  244.1 43.2 %all-gather.6.cloned.1.call-done = bf16[512,4096]{1,0:T(8,128)(2,1)} async-done(((bf16[512,512]{1,0:T(8,128)(2,1)}), bf16[512,4096]{1,0:T(8,128)(2,1)}) %all-gather.6.cloned.1.call-update) | async-done | bytes 4194320 | tf_op jit(solution)/shard_map/all_gather | solution.py:40
  287.3 17.1 %bitcast_add_fusion = f32[5120,512]{0,1:T(8,128)} fusion(f32[5120,512]{0,1:T(8,128)} %fusion, bf16[512,5120]{1,0:T(8,128)(2,1)} %param.5, bf16[512,4096]{1,0:T(8,128)(2,1)} %all-gather.6.cloned.1.call-done, bf16[4096,512]{1,0:T(8,128)(2,1)} %all-gather.8.cloned.1.call-done), kind=kOutput, calls=%fused_computation | convolution fusion | flops 4834721792 | bytes 34603008 | tf_op jit(solution)/shard_map/dot_general | solution.py:12
  304.5 11.4 %copy.13 = f32[5120,512]{1,0:T(8,128)} copy(f32[5120,512]{0,1:T(8,128)} %bitcast_add_fusion) | data formatting | bytes 20971520
  315.9 111.0 %reduce-scatter.7.cloned.1.call-done = f32[320,512]{1,0:T(8,128)} async-done(((f32[5120,512]{1,0:T(8,128)}), f32[320,512]{1,0:T(8,128)}) %reduce-scatter.7.cloned.1.call-update) | async-done | bytes 655376 | tf_op jit(solution)/shard_map/reduce_scatter | solution.py:44
  426.9 1.3 copy.14
  428.3 0.8 multiply_reduce_fusion
  429.1 64.5 %psum.7 = f32[]{:T(128)} all-reduce(f32[]{:T(128)} %multiply_reduce_fusion), channel_id=1, replica_groups=mesh['fsdp'=16,'tp'=8] {'fsdp','tp'}, use_global_device_ids=true, to_apply=%region_3.4 | all-reduce | flops 1 | bytes 8 | tf_op jit(solution)/shard_map/psum | solution.py:50
  494.3 1.9 multiply_convert_fusion
  (4 shorter events, 0.0 us)
Async XLA Ops:
  6.5 61.8 %all-gather.8.cloned.1.call-start = ((), (), s32[]{:S(2)}) async-start(), calls=%async_computation.4 | async-start | bytes 4456448 | tf_op jit(solution)/shard_map/all_gather | solution.py:28
  7.3 122.0 %all-gather.4.cloned.1.call-start = ((), (), s32[]{:S(2)}) async-start(), calls=%async_computation.2 | async-start | bytes 5570560 | tf_op jit(solution)/shard_map/all_gather | solution.py:27
  8.0 226.4 %reduce-scatter.5.cloned.1.call-start = ((), (), s32[]{:S(2)}) async-start(), calls=%async_computation.5 | async-start | bytes 9437184 | tf_op jit(solution)/shard_map/reduce_scatter | solution.py:36
  142.8 0.7 copy-start
  142.8 144.5 %all-gather.6.cloned.1.call-start = ((), (), s32[]{:S(2)}) async-start(), calls=%async_computation.3 | async-start | bytes 4718592 | tf_op jit(solution)/shard_map/all_gather | solution.py:40
  151.4 275.6 %reduce-scatter.7.cloned.1.call-start = ((), (), s32[]{:S(2)}) async-start(), calls=%async_computation.6 | async-start | bytes 11141120 | tf_op jit(solution)/shard_map/reduce_scatter | solution.py:44
Sparse Core Ops, SparseCore 0:
  9.8 58.4 all-gather.7
  70.7 58.5 all-gather.3
  143.0 91.3 reduce-scatter.4
  235.9 51.3 all-gather.5
  316.0 110.8 reduce-scatter.6
where the time goes:
time: 504 us; the launch traced here: 503 us
  waiting for transfers between devices  360 us (71%)
  blocking collectives  64.5 us (13%)
  matrix products  48.2 us (10%)
  between operations  13.8 us (3%)
  local copies, waits for them, and re-layouts  13.3 us (3%)
    reduce_scatter x1, waiting for transfers between devices, per_device(): lax.psum_scatter(contract_tokens(activations, delta_cols) + contract_toke...  111 us
    reduce_scatter x1, waiting for transfers between devices, per_device(): lax.psum_scatter(contract_last(forward_cols, proxy_cols), 'tp', scatter_d...  82.8 us
    psum x1, blocking collectives, per_device(): total = lax.psum(jnp.sum(grad_block * grad_block), ('fsdp', 'tp'))  64.5 us
    all_gather x1, waiting for transfers between devices, per_device(): lax.all_gather(grow_operator, 'fsdp', axis=0, tiled=True)  61 us
    all_gather x1, waiting for transfers between devices, per_device(): lax.all_gather(proxy_weight, 'fsdp', axis=0, tiled=True)  60.2 us
    all_gather x1, waiting for transfers between devices, per_device(): back_all = lax.all_gather(back_cols, 'tp', axis=1, tiled=True)  43.2 us
    dot_general x2, matrix products, contract_tokens(): lax.dot_general(left, right, (((0,), (0,)), ((), ())), preferred_element_...  26.9 us
    dot_general x1, matrix products, contract_last(): lax.dot_general(left, right, (((1,), (1,)), ((), ())), preferred_element_...  13.5 us
  transfers between devices with their start and end apart: 5, of which 5 were waited for; matrix products, arithmetic and copies ran while one was open for 4% of the time, Pallas kernels for 0%

commit v1 on v0

v1 whole, which is shorter than its diff:
```python
import jax
import jax.numpy as jnp
from jax import lax
from jax.experimental import pallas as pl
from jax.experimental.pallas import tpu as pltpu
from jax.sharding import PartitionSpec as P

MESH = pl.DeviceIdType.MESH
F32, BF16 = jnp.float32, jnp.bfloat16

D = 5120
PD = 4096
LEN = 256
ROWS = 512
WR = 320
VR = 256
CT = 512
NC = 2
CW = CT // NC
NX = 4
NY = 4

G_Z, G_XP, G_XM, G_FP, G_FM, G_S, G_N = 0, 1, 3, 5, 6, 7, 15
T_Z, T_YP, T_YM, T_FP, T_FM, T_N = 0, 1, 3, 5, 6, 7
R_PF, R_PD, R_MF, R_MD, R_P2, R_M2, R_Z, R_C, R_N = 0, 1, 2, 3, 4, 5, 6, 7, 8
K_W = 0
K_V = K_W + NC * G_N
K_B = K_V + G_N
K_P = K_B + NC * T_N
K_G = K_P + NC * R_N
K_S = K_G + NC * R_N
K_N = K_S + 10


def dot(a, b):
    return jnp.dot(a, b, preferred_element_type=F32)


def dot_t(a, b):
    return lax.dot_general(a, b, (((1,), (1,)), ((), ())), preferred_element_type=F32)


def kernel(
    a_hbm, g_hbm, w_hbm, v_hbm, len_ref, out_ref,
    av, gv, at, gt, w0, w1, vg, bg, fw, dl, pp, ps, pr1, pr2, prz, gsib, gcore, gown, gs, gr1, gr2, grz,
    acc, sc, local, ss, rs,
):
    f = lax.axis_index("fsdp")
    t = lax.axis_index("tp")
    x, zh, core = f // 4, (f // 2) % 2, f % 2
    zl, y = t // 4, t % 4

    def fid(dx, r, other_core=0):
        c = core if other_core == 0 else 1 - core
        z = zh if r == 0 else 1 - zh
        return ((x + dx) % NX) * 4 + z * 2 + c

    def tid(dy, r):
        z = zl if r == 0 else 1 - zl
        return z * NY + (y + dy) % NY

    z_dev, sib = (fid(0, 1), t), (fid(0, 0, 1), t)
    xp, xm, x2 = (fid(1, 0), t), (fid(3, 0), t), (fid(2, 0), t)
    zl_dev = (f, tid(0, 1))
    yp, ym, y2 = (f, tid(1, 0)), (f, tid(3, 0)), (f, tid(2, 0))
    zd_dev = (fid(0, 1), tid(0, 1))
    peers = (z_dev, sib, xp, xm, x2, zl_dev, yp, ym, y2, zd_dev)

    load_a = pltpu.make_async_copy(a_hbm, av, local.at[0])
    load_g = pltpu.make_async_copy(g_hbm, gv, local.at[1])
    load_a.start()
    load_g.start()
    wg = (w0, w1)

    def wrows(src):
        return pl.ds(pl.multiple_of(src * WR, 64), WR)

    def vrows(src):
        return pl.ds(pl.multiple_of(src * VR, VR), VR)

    load_w = []
    for c in range(NC):
        load_w.append(
            pltpu.make_async_copy(w_hbm.at[:, pl.ds(c * CW, CW)], wg[c].at[wrows(f)], local.at[2 + c])
        )
    load_w.append(pltpu.make_async_copy(v_hbm, vg.at[vrows(f)], local.at[2 + NC]))
    for load in load_w:
        load.start()

    barrier = pltpu.get_barrier_semaphore()
    for peer in peers:
        pl.semaphore_signal(barrier, inc=1, device_id=peer, device_id_type=MESH)
    pl.semaphore_wait(barrier, len(peers))

    sent = []

    def remote(src, dst, k, dev):
        return pltpu.make_async_remote_copy(
            src_ref=src, dst_ref=dst, send_sem=ss.at[k], recv_sem=rs.at[k], device_id=dev, device_id_type=MESH
        )

    def send(src, dst, k, dev):
        copy = remote(src, dst, k, dev)
        copy.start()
        sent.append(copy)

    def arrived(dst, k):
        remote(dst, dst, k, sib).wait_recv()

    class Gather:
        def __init__(self, own, place, k):
            self.own, self.place, self.k = own, place, k

        def start(self):
            own, dst, k = self.own, self.place(f), self.k
            send(own, dst, k + G_Z, z_dev)
            send(own, dst, k + G_XP, xp)
            send(own, dst, k + G_XM, xm)
            send(own, dst, k + G_S, sib)

        def take_z(self):
            ref, k = self.place(fid(0, 1)), self.k
            arrived(ref, k + G_Z)
            send(ref, ref, k + G_XP + 1, xp)
            send(ref, ref, k + G_XM + 1, xm)
            send(ref, ref, k + G_S + 1, sib)

        def take_x(self, r):
            k = self.k
            back_ref, ahead_ref = self.place(fid(3, r)), self.place(fid(1, r))
            arrived(back_ref, k + G_XP + r)
            if r == 0:
                send(back_ref, back_ref, k + G_FP, xp)
            send(back_ref, back_ref, k + G_S + 6 + r, sib)
            arrived(ahead_ref, k + G_XM + r)
            if r == 1:
                send(ahead_ref, ahead_ref, k + G_FM, xm)
            send(ahead_ref, ahead_ref, k + G_S + 2 + r, sib)

        def take_far(self, r):
            k = self.k
            ref = self.place(fid(2, r))
            arrived(ref, k + (G_FP if r == 0 else G_FM))
            send(ref, ref, k + G_S + 4 + r, sib)

        def take_sib(self):
            for dx in range(NX):
                for r in range(2):
                    arrived(self.place(fid(dx, r, 1)), self.k + G_S + 2 * dx + r)

    def w_place(c):
        return lambda src: wg[c].at[wrows(src)]

    gw = [Gather(w_hbm.at[:, pl.ds(c * CW, CW)], w_place(c), K_W + c * G_N) for c in range(NC)]
    gvv = Gather(v_hbm, lambda src: vg.at[vrows(src)], K_V)

    def turn(src, dst, first, count):
        @pl.loop(first, first + count)
        def _(j):
            at_col = pl.multiple_of(j * 128, 128)
            dst[pl.ds(at_col, 128), :] = src[:, pl.ds(at_col, 128)].T

    gw[0].start()
    gw[1].start()
    load_a.wait()
    turn(av, at, 0, 20)
    gw[0].take_z()
    turn(av, at, 20, 20)
    gw[0].take_x(0)
    gw[1].take_z()
    gvv.start()
    load_g.wait()
    turn(gv, gt, 0, 20)
    gw[0].take_x(1)
    gw[1].take_x(0)
    turn(gv, gt, 20, 20)
    gw[0].take_far(0)
    gw[0].take_far(1)
    gvv.take_z()
    for load in load_w:
        load.wait()
    gw[0].take_sib()

    row_of = lax.broadcasted_iota(jnp.int32, (LEN, CW), 0)

    def keep(j, block):
        return jnp.where(row_of < len_ref[j], block, jnp.zeros_like(block))

    own_col = pl.multiple_of(t * CT, CT)

    def bcols(src, c):
        return bg.at[:, pl.ds(pl.multiple_of(src * CT + c * CW, CW), CW)]

    def project(c):
        @pl.loop(0, ROWS // LEN)
        def _(j):
            r0 = pl.ds(pl.multiple_of(j * LEN, LEN), LEN)
            block = dot(gv[r0, :], wg[c][...]).astype(BF16)
            bg[r0, pl.ds(pl.multiple_of(own_col + c * CW, CW), CW)] = keep(j, block)

        own = bcols(t, c)
        k = K_B + c * T_N
        send(own, own, k + T_Z, zl_dev)
        send(own, own, k + T_YP, yp)
        send(own, own, k + T_YM, ym)

        @pl.loop(0, ROWS // LEN)
        def _(j):
            r0 = pl.ds(pl.multiple_of(j * LEN, LEN), LEN)
            fw[r0, c * CW : (c + 1) * CW] = dot(av[r0, :], wg[c][...]).astype(BF16)

    def back_z(c):
        ref, k = bcols(tid(0, 1), c), K_B + c * T_N
        arrived(ref, k + T_Z)
        send(ref, ref, k + T_YP + 1, yp)
        send(ref, ref, k + T_YM + 1, ym)

    def back_y(c):
        k = K_B + c * T_N
        ref = bcols(tid(3, 0), c)
        arrived(ref, k + T_YP)
        send(ref, ref, k + T_FP, yp)
        ref = bcols(tid(1, 1), c)
        arrived(ref, k + T_YM + 1)
        send(ref, ref, k + T_FM, ym)

    def back_end(c):
        k = K_B + c * T_N
        arrived(bcols(tid(1, 0), c), k + T_YM)
        arrived(bcols(tid(3, 1), c), k + T_YP + 1)
        arrived(bcols(tid(2, 0), c), k + T_FP)
        arrived(bcols(tid(2, 1), c), k + T_FM)

    project(0)
    gw[1].take_x(1)
    gw[1].take_far(0)
    gw[1].take_far(1)
    gvv.take_x(0)
    back_z(0)
    gw[1].take_sib()
    project(1)
    gvv.take_x(1)
    back_y(0)
    gvv.take_far(0)
    gvv.take_far(1)
    back_z(1)
    gvv.take_sib()

    def partial_out(s):
        @pl.loop(0, 2 * NY)
        def _(i):
            dy, r = (i // 2 + 2) % NY, i % 2
            dest = ((zl + r) % 2) * NY + (y + dy) % NY
            rows = pl.ds(pl.multiple_of(dest * CT + s * CW, CW), CW)
            ps[s, 2 * dy + r] = dot_t(fw[...], vg[rows, :]).astype(BF16)

    class Sum:
        def __init__(self, blocks, near, far, zbuf, k, plus, minus, across):
            self.blocks, self.near, self.far, self.zbuf, self.k = blocks, near, far, zbuf, k
            self.plus, self.minus, self.across = plus, minus, across

        def start(self):
            k = self.k
            send(self.blocks.at[4], self.near.at[0], k + R_PF, self.plus)
            send(self.blocks.at[5], self.near.at[1], k + R_MF, self.minus)
            send(self.blocks.at[3], self.far.at[0], k + R_PD, self.plus)
            send(self.blocks.at[6], self.far.at[1], k + R_MD, self.minus)

        def middle(self):
            k = self.k
            for mine, slot, far, sem, out, dev in (
                (2, 0, 2, R_PF, R_P2, self.plus),
                (7, 1, 3, R_MF, R_M2, self.minus),
            ):
                arrived(self.near.at[slot], k + sem)
                self.blocks[mine] = (self.blocks[mine].astype(F32) + self.near[slot].astype(F32)).astype(BF16)
                send(self.blocks.at[mine], self.far.at[far], k + out, dev)

        def end(self, own, other):
            k = self.k
            arrived(self.far.at[0], k + R_PD)
            arrived(self.far.at[3], k + R_M2)
            self.blocks[1] = (other() + self.far[0].astype(F32) + self.far[3].astype(F32)).astype(BF16)
            send(self.blocks.at[1], self.zbuf, k + R_Z, self.across)
            arrived(self.far.at[1], k + R_MD)
            arrived(self.far.at[2], k + R_P2)
            acc[0 : own.shape[0], :] = own[...].astype(F32) + self.far[1].astype(F32) + self.far[2].astype(F32)

        def last(self, rows):
            arrived(self.zbuf, self.k + R_Z)
            return acc[0:rows, :] + self.zbuf[...].astype(F32)

    psum = [
        Sum(ps.at[s], pr1.at[s], pr2.at[s], prz.at[s], K_P + s * R_N, yp, ym, zl_dev) for s in range(NC)
    ]
    gsum = [
        Sum(gs.at[s], gr1.at[s], gr2.at[s], grz.at[s], K_G + s * R_N, xp, xm, z_dev) for s in range(NC)
    ]

    def finish_out(s):
        total = psum[s].last(ROWS).astype(BF16)
        for j in range(ROWS // LEN):
            pp[j * LEN : (j + 1) * LEN, s * CW : (s + 1) * CW] = keep(j, total[j * LEN : (j + 1) * LEN])

    def grad_block(i, s, c):
        dest = ((x + i // 2) % NX) * 4 + ((zh + i % 2) % 2) * 2 + c
        cols = slice(s * CW, (s + 1) * CW)
        return dot(at[wrows(dest), :], dl[:, cols]) + dot(gt[wrows(dest), :], pp[:, cols])

    def gradient(s):
        @pl.loop(0, 2 * NX)
        def _(i):
            gsib[s, i] = grad_block(i, s, 1 - core).astype(BF16)

        send(gsib.at[s], gcore.at[s], K_G + s * R_N + R_C, sib)

        @pl.loop(0, 2 * NX)
        def _(i):
            gown[i] = grad_block(i, s, core)

        arrived(gcore.at[s], K_G + s * R_N + R_C)

        @pl.loop(0, 2 * NX)
        def _(i):
            whole = gown[i] + gcore[s, i].astype(F32)
            gown[i] = whole
            gs[s, i] = whole.astype(BF16)

        gsum[s].start()

    partial_out(0)
    psum[0].start()
    partial_out(1)
    psum[1].start()
    back_y(1)
    back_end(0)
    back_end(1)
    psum[0].middle()
    for s in range(NC):
        cols = slice(s * CW, (s + 1) * CW)
        dl[:, cols] = dot(bg[...], vg[:, cols]).astype(BF16)
    psum[1].middle()
    psum[0].end(ps.at[0, 0], lambda: ps[0, 1].astype(F32))
    finish_out(0)
    gradient(0)
    psum[1].end(ps.at[1, 0], lambda: ps[1, 1].astype(F32))
    gsum[0].middle()
    finish_out(1)
    gsum[0].end(gown.at[0], lambda: gown[1])
    out0 = gsum[0].last(WR)
    res0 = out0
    sc_part = jnp.sum((out0 * out0).reshape(WR // 8, 8, CW), axis=0)
    gradient(1)
    gsum[1].middle()
    gsum[1].end(gown.at[0], lambda: gown[1])
    out1 = gsum[1].last(WR)
    sc_part = sc_part + jnp.sum((out1 * out1).reshape(WR // 8, 8, CW), axis=0)
    sc[0] = sc_part[:, 0:128] + sc_part[:, 128:256]

    send(sc.at[0], sc.at[1], K_S, sib)
    arrived(sc.at[1], K_S)
    sc[2] = sc[0] + sc[1]
    base, slot = 2, 1
    for devs in ((xp, xm, x2), (zl_dev, z_dev, zd_dev), (yp, ym, y2)):
        for j in range(3):
            send(sc.at[base], sc.at[base + 1 + j], K_S + slot + j, devs[j])
        for j in range(3):
            arrived(sc.at[base + 1 + j], K_S + slot + j)
        sc[base + 4] = (sc[base] + sc[base + 1]) + (sc[base + 2] + sc[base + 3])
        base, slot = base + 4, slot + 3
    scale = lax.rsqrt(jnp.sum(sc[base]) / (D * PD) + 1e-6)
    out_ref[:, 0:CW] = (res0 * scale).astype(BF16)
    out_ref[:, CW:CT] = (out1 * scale).astype(BF16)
    for copy in sent:
        copy.wait_send()


def per_device(activations, cotangent, lengths, grow_operator, proxy_weight):
    anywhere = pl.BlockSpec(memory_space=pl.ANY)
    return pl.pallas_call(
        kernel,
        out_shape=jax.ShapeDtypeStruct((WR, CT), BF16),
        in_specs=[anywhere] * 4 + [pl.BlockSpec(memory_space=pltpu.SMEM)],
        out_specs=pl.BlockSpec(memory_space=pltpu.VMEM),
        scratch_shapes=[
            pltpu.VMEM((ROWS, D), BF16),
            pltpu.VMEM((ROWS, D), BF16),
            pltpu.VMEM((D, ROWS), BF16),
            pltpu.VMEM((D, ROWS), BF16),
            pltpu.VMEM((D, CW), BF16),
            pltpu.VMEM((D, CW), BF16),
            pltpu.VMEM((PD, CT), BF16),
            pltpu.VMEM((ROWS, PD), BF16),
            pltpu.VMEM((ROWS, CT), BF16),
            pltpu.VMEM((ROWS, CT), BF16),
            pltpu.VMEM((ROWS, CT), BF16),
            pltpu.VMEM((NC, 2 * NY, ROWS, CW), BF16),
            pltpu.VMEM((NC, 2, ROWS, CW), BF16),
            pltpu.VMEM((NC, 4, ROWS, CW), BF16),
            pltpu.VMEM((NC, ROWS, CW), BF16),
            pltpu.VMEM((NC, 2 * NX, WR, CW), BF16),
            pltpu.VMEM((NC, 2 * NX, WR, CW), BF16),
            pltpu.VMEM((2 * NX, WR, CW), F32),
            pltpu.VMEM((NC, 2 * NX, WR, CW), BF16),
            pltpu.VMEM((NC, 2, WR, CW), BF16),
            pltpu.VMEM((NC, 4, WR, CW), BF16),
            pltpu.VMEM((NC, WR, CW), BF16),
            pltpu.VMEM((ROWS, CW), F32),
            pltpu.VMEM((15, 8, 128), F32),
            pltpu.SemaphoreType.DMA((3 + NC,)),
            pltpu.SemaphoreType.DMA((K_N,)),
            pltpu.SemaphoreType.DMA((K_N,)),
        ],
        compiler_params=pltpu.CompilerParams(
            collective_id=0, has_side_effects=True, vmem_limit_bytes=63 * 1024 * 1024
        ),
    )(activations, cotangent, grow_operator, proxy_weight, lengths)


def solution(mesh):
    placed = (P("fsdp", None), P("fsdp", None), P("fsdp"), P("fsdp", "tp"), P("fsdp", "tp"))
    return jax.shard_map(
        per_device, mesh=mesh, in_specs=placed, out_specs=P("fsdp", "tp"), check_vma=False
    )
```

time: 504 us -> 176 us (0.35)
  waiting for transfers between devices: 360 us -> 0 us
  Pallas kernels: 0 us -> 174 us
  blocking collectives: 64.5 us -> 0 us
  matrix products: 48.2 us -> 0 us
  between operations: 13.8 us -> 0.01 us
  local copies, waits for them, and re-layouts: 13.3 us -> 1.72 us
    reduce_scatter x2 -> x0, waiting for transfers between devices: 194 us -> none  [the longest x1 111 us: per_device(): lax.psum_scatter(contract_tokens(activations, delta_cols) + contract_toke...]
    pallas_call x0 -> x1, Pallas kernels: none -> 174 us  [per_device(): pl.pallas_call(kernel, out_shape=jax.ShapeDtypeStruct((WR, CT), BF16), in...]
    all_gather x3 -> x0, waiting for transfers between devices: 164 us -> none  [the longest x1 61 us: per_device(): lax.all_gather(grow_operator, 'fsdp', axis=0, tiled=True)]
    psum x1 -> x0, blocking collectives: 64.5 us -> none  [per_device(): total = lax.psum(jnp.sum(grad_block * grad_block), ('fsdp', 'tp'))]
    dot_general x4 -> x0, matrix products: 48.2 us -> none  [the longest x2 26.9 us: contract_tokens(): lax.dot_general(left, right, (((0,), (0,)), ((), ())), preferred_element_...]
    unnamed x4 -> x1, local copies, waits for them, and re-layouts: 13.3 us -> 1.72 us
  transfers between devices with their start and end apart: 5 -> 0, of which waited for: 5 -> 0; matrix products, arithmetic and copies ran while one was open for 4% -> 0% of each run, Pallas kernels for 0% -> 0%
where the time goes in v1:
time: 176 us; the launch traced here: 175 us
  Pallas kernels  174 us (99%)
    pallas_call x1, Pallas kernels, per_device(): pl.pallas_call(kernel, out_shape=jax.ShapeDtypeStruct((WR, CT), BF16), in...  174 us

profile of v1, /device:TPU:0, one launch (start us, length us, event | category | flops | bytes accessed | tf_op | source)
XLA Modules:
  0.0 175.4 jit_solution(11771715555217084948)
XLA Ops:
  0.0 173.6 %shard_map.55 = bf16[320,512]{1,0:T(8,128)(2,1)} custom-call(bf16[512,5120]{1,0:T(8,128)(2,1)} %a_hbm.1, bf16[512,5120]{1,0:T(8,128)(2,1)} %g_hbm.1, bf16[320,512]{1,0:T(8,128)(2,1)} %w_hbm.1, bf16[256,512]{1,0:T(8,128)(2,1)} %v_hbm.1, s32[2]{0:T(128)} %len_ref.1), custom_call_target="tpu_custom_call" | custom-call | tf_op jit(solution)/shard_map/pallas_call | solution.py:380
  173.6 1.7 copy.7

commit v2 on v0

v2 whole, which is shorter than its diff:
```python
import jax
import jax.numpy as jnp
from jax import lax
from jax.experimental import pallas as pl
from jax.experimental.pallas import tpu as pltpu
from jax.sharding import PartitionSpec as P

MESH = pl.DeviceIdType.MESH
F32, BF16 = jnp.float32, jnp.bfloat16

D = 5120
PD = 4096
LEN = 256
ROWS = 512
WR = 320
VR = 256
CT = 512
NX = 4
NY = 4

WP = ((0, 128), (128, 128), (256, 256))
GP = ((0, 128), (128, 128), (256, 128), (384, 128))
ROUTE_B = "zzz"
ROUTE_P = "zyyz"
EARLY = (0, 1, 1, 1)
SEMS = 192

ORDER = (
    "w0.start", "w1.start", "w0.a0", "w0.b0", "w0.z", "ta0", "w1.a0", "w1.b0",
    "w1.z", "w2.start", "ta1", "ta2", "w0.a1", "w0.f0", "ta3", "w0.b1",
    "w1.a1", "tg0", "tg1", "w1.f0", "w2.z", "v.start", "tg2", "w1.b1",
    "w2.a0", "tg3", "w0.f1", "w0.sib", "b0.proj", "w1.f1", "w2.b0", "b0.fwd",
    "w1.sib", "b1.proj", "w2.a1", "w2.b1", "b1.fwd", "b0.yb", "b0.z", "v.z",
    "b1.yb", "b1.z", "v.a0", "v.b0", "b0.ya", "w2.f0", "w2.f1", "w2.sib",
    "b1.ya", "b2.proj", "b2.fwd", "b0.end", "v.a1", "v.b1", "b1.end", "b2.z",
    "v.f0", "v.f1", "b2.yb", "v.sib", "p0.part", "p1.part", "b2.ya", "p2.part",
    "p0.mm", "p3.part", "p0.mp", "b2.end", "delta", "p1.zm", "p0.eo", "p3.mp",
    "g1.pre", "p3.mm", "g2.pre", "p1.mm", "p1.mp", "g3.pre", "p2.zm", "p3.eo",
    "p1.last", "p0.last", "g0.sb", "g0.ow", "g0.comb", "g1.sb", "g1.ow", "g0.mm",
    "g0.mp", "p2.mm", "p2.mp", "p3.last", "g1.comb", "g0.eo", "p2.last", "g2.sb",
    "g0.last", "g1.mm", "g1.mp", "g2.ow", "g2.comb", "g3.sb", "g1.eo", "g3.ow",
    "g2.mm", "g2.mp", "g3.comb", "g1.last", "g2.eo", "g3.mm", "g3.mp", "g2.last",
    "g3.eo", "g3.last",
)


def dot(a, b):
    return jnp.dot(a, b, preferred_element_type=F32)


def dot_t(a, b):
    return lax.dot_general(a, b, (((1,), (1,)), ((), ())), preferred_element_type=F32)


def up(value):
    return value.astype(F32)


def kernel(a_hbm, g_hbm, w_hbm, v_hbm, len_ref, out_ref, *scratch):
    scratch = list(scratch)
    av, gv, at, gt, vg, bg, fw, dl, pp, res, sc, local, ss, rs = scratch[:14]
    del scratch[:14]

    def take(count):
        got = scratch[:count]
        del scratch[:count]
        return got

    wg = take(len(WP))
    ps, pnear, pfar, pz = (take(len(GP)) for _ in range(4))
    gsib, gcore, gown, gs, gnear, gfar, gz = (take(len(GP)) for _ in range(7))
    gpre = take(len(GP))

    f = lax.axis_index("fsdp")
    t = lax.axis_index("tp")
    x, zh, core = f // 4, (f // 2) % 2, f % 2
    zl, y = t // 4, t % 4

    def fid(dx, r, other_core=0):
        c = core if other_core == 0 else 1 - core
        z = zh if r == 0 else 1 - zh
        return ((x + dx) % NX) * 4 + z * 2 + c

    def tid(dy, r):
        z = zl if r == 0 else 1 - zl
        return z * NY + (y + dy) % NY

    z_dev, sib = (fid(0, 1), t), (fid(0, 0, 1), t)
    xp, xm, x2 = (fid(1, 0), t), (fid(3, 0), t), (fid(2, 0), t)
    xps, xms, x2s = (fid(1, 0, 1), t), (fid(3, 0, 1), t), (fid(2, 0, 1), t)
    zl_dev = (f, tid(0, 1))
    yp, ym, y2 = (f, tid(1, 0)), (f, tid(3, 0)), (f, tid(2, 0))
    zd_dev = (fid(0, 1), tid(0, 1))
    peers = (z_dev, sib, xp, xm, x2, xps, xms, x2s, zl_dev, yp, ym, y2, zd_dev)

    def wrows(src):
        return pl.ds(pl.multiple_of(src * WR, 64), WR)

    def vrows(src):
        return pl.ds(pl.multiple_of(src * VR, VR), VR)

    loads = [
        pltpu.make_async_copy(a_hbm, av, local.at[0]),
        pltpu.make_async_copy(g_hbm, gv, local.at[1]),
        pltpu.make_async_copy(v_hbm, vg.at[vrows(f)], local.at[2]),
    ]
    load_w = [
        pltpu.make_async_copy(w_hbm.at[:, pl.ds(first, width)], wg[c].at[wrows(f)], local.at[3 + c])
        for c, (first, width) in enumerate(WP)
    ]
    for load in loads + load_w:
        load.start()

    barrier = pltpu.get_barrier_semaphore()
    for peer in peers:
        pl.semaphore_signal(barrier, inc=1, device_id=peer, device_id_type=MESH)
    pl.semaphore_wait(barrier, len(peers))

    sent, sems, steps = [], {}, {}

    def remote(src, dst, key, dev):
        k = sems.setdefault(key, len(sems))
        return pltpu.make_async_remote_copy(
            src_ref=src, dst_ref=dst, send_sem=ss.at[k], recv_sem=rs.at[k], device_id=dev, device_id_type=MESH
        )

    def send(src, dst, key, dev):
        copy = remote(src, dst, key, dev)
        copy.start()
        sent.append(copy)

    def arrived(dst, key):
        remote(dst, dst, key, sib).wait_recv()

    def step(name, run, *args):
        steps[name] = lambda: run(*args)

    def turn(src, dst, quarter):
        if quarter == 0:
            loads[0 if src is av else 1].wait()
        part = D // 128 // 4

        @pl.loop(quarter * part, (quarter + 1) * part)
        def _(j):
            col = pl.multiple_of(j * 128, 128)
            dst[pl.ds(col, 128), :] = src[:, pl.ds(col, 128)].T

    for quarter in range(4):
        step(f"ta{quarter}", turn, av, at, quarter)
        step(f"tg{quarter}", turn, gv, gt, quarter)

    def gather(n, own, place, load):
        def start():
            dst = place(f)
            send(own, dst, (n, "z"), z_dev)
            send(own, dst, (n, "p", 0), xp)
            send(own, dst, (n, "m", 0), xm)
            send(own, dst, (n, "s", 0, 0), sib)

        def over_z():
            ref = place(fid(0, 1))
            arrived(ref, (n, "z"))
            send(ref, ref, (n, "p", 1), xp)
            send(ref, ref, (n, "m", 1), xm)
            send(ref, ref, (n, "s", 0, 1), sib)

        def behind(r):
            ref = place(fid(3, r))
            arrived(ref, (n, "p", r))
            if r == 0:
                send(ref, ref, (n, "f", 0), xp)
            send(ref, ref, (n, "s", 3, r), sib)

        def ahead(r):
            ref = place(fid(1, r))
            arrived(ref, (n, "m", r))
            if r == 1:
                send(ref, ref, (n, "f", 1), xm)
            send(ref, ref, (n, "s", 1, r), sib)

        def far(r):
            ref = place(fid(2, r))
            arrived(ref, (n, "f", r))
            send(ref, ref, (n, "s", 2, r), sib)

        def end():
            load.wait()
            for dx in range(NX):
                for r in range(2):
                    arrived(place(fid(dx, r, 1)), (n, "s", dx, r))

        step(f"{n}.start", start)
        step(f"{n}.z", over_z)
        for r in range(2):
            step(f"{n}.b{r}", behind, r)
            step(f"{n}.a{r}", ahead, r)
            step(f"{n}.f{r}", far, r)
        step(f"{n}.sib", end)

    def w_place(c):
        return lambda src: wg[c].at[wrows(src)]

    for c, (first, width) in enumerate(WP):
        gather(f"w{c}", w_hbm.at[:, pl.ds(first, width)], w_place(c), load_w[c])
    gather("v", v_hbm, lambda src: vg.at[vrows(src)], loads[2])

    def keep(j, block):
        row_of = lax.broadcasted_iota(jnp.int32, block.shape, 0)
        return jnp.where(row_of < len_ref[j], block, jnp.zeros_like(block))

    halves = (slice(0, LEN), slice(LEN, ROWS))

    def back(c):
        first, width = WP[c]
        n, route = f"b{c}", ROUTE_B[c]

        def cols(src):
            return pl.ds(pl.multiple_of(src * CT + first, 128), width)

        def block(dy, r):
            return bg.at[:, cols(tid(dy, r))]

        def half(dy, j):
            return bg.at[pl.ds(j * LEN, LEN), cols(tid(dy, 0))]

        def project():
            @pl.loop(0, ROWS // LEN)
            def _(j):
                r0 = pl.ds(pl.multiple_of(j * LEN, LEN), LEN)
                bg[r0, cols(t)] = keep(j, dot(gv[r0, :], wg[c][...]).astype(BF16))

            own = block(0, 0)
            if route == "z":
                send(own, own, (n, "z", 0), zl_dev)
            send(own, own, (n, "p", 0), yp)
            send(own, own, (n, "m", 0), ym)
            if route == "y":
                send(own, own, (n, "z", 0), zl_dev)

        def forward():
            @pl.loop(0, ROWS // LEN)
            def _(j):
                r0 = pl.ds(pl.multiple_of(j * LEN, LEN), LEN)
                fw[r0, first : first + width] = dot(av[r0, :], wg[c][...]).astype(BF16)

        def z_first():
            ref = block(0, 1)
            arrived(ref, (n, "z", 0))
            send(ref, ref, (n, "p", 1), yp)
            send(ref, ref, (n, "m", 1), ym)

        def behind():
            ref = block(3, 0)
            arrived(ref, (n, "p", 0))
            if route == "z":
                send(ref, ref, (n, "f", 0), yp)
            else:
                part = half(3, 0)
                send(part, part, (n, "f", 0), yp)
                send(ref, ref, (n, "z", 3), zl_dev)

        def ahead():
            if route == "z":
                ref = block(1, 1)
                arrived(ref, (n, "m", 1))
                send(ref, ref, (n, "f", 1), ym)
            else:
                ref, part = block(1, 0), half(1, 1)
                arrived(ref, (n, "m", 0))
                send(part, part, (n, "f", 1), ym)
                send(ref, ref, (n, "z", 1), zl_dev)

        def z_last():
            arrived(half(2, 0), (n, "f", 0))
            arrived(half(2, 1), (n, "f", 1))
            ref = block(2, 0)
            send(ref, ref, (n, "z", 2), zl_dev)

        def end():
            if route == "z":
                arrived(block(1, 0), (n, "m", 0))
                arrived(block(3, 1), (n, "p", 1))
                arrived(block(2, 0), (n, "f", 0))
                arrived(block(2, 1), (n, "f", 1))
            else:
                for dy in range(NY):
                    arrived(block(dy, 1), (n, "z", dy))

        step(f"{n}.proj", project)
        step(f"{n}.fwd", forward)
        step(f"{n}.z", z_first if route == "z" else z_last)
        step(f"{n}.yb", behind)
        step(f"{n}.ya", ahead)
        step(f"{n}.end", end)

    for c in range(len(WP)):
        back(c)

    def map_back():
        for first in range(0, CT, 256):
            dl[:, first : first + 256] = dot(bg[...], vg[:, first : first + 256]).astype(BF16)

    step("delta", map_back)

    def ring_sum(n, blocks, near, far, zbuf, plus, minus, across, own, other, finish):
        def start():
            send(blocks.at[4], near.at[0], (n, "pf"), plus)
            send(blocks.at[5], near.at[1], (n, "mf"), minus)
            send(blocks.at[3], far.at[0], (n, "pd"), plus)
            send(blocks.at[6], far.at[1], (n, "md"), minus)

        def through(mine, slot, key, to, out, dev):
            arrived(near.at[slot], (n, key))
            blocks[mine] = (up(blocks[mine]) + up(near[slot])).astype(BF16)
            send(blocks.at[mine], far.at[to], (n, out), dev)

        def end_other():
            arrived(far.at[0], (n, "pd"))
            arrived(far.at[3], (n, "m2"))
            blocks[1] = (up(other()) + up(far[0]) + up(far[3])).astype(BF16)
            send(blocks.at[1], zbuf, (n, "z"), across)

        def last():
            arrived(far.at[1], (n, "md"))
            arrived(far.at[2], (n, "p2"))
            arrived(zbuf, (n, "z"))
            finish((up(own()) + up(far[1])) + (up(far[2]) + up(zbuf[...])))

        step(f"{n}.mp", through, 2, 0, "pf", 2, "p2", plus)
        step(f"{n}.mm", through, 7, 1, "mf", 3, "m2", minus)
        step(f"{n}.eo", end_other)
        step(f"{n}.last", last)
        return start

    def cross_sum(n, blocks, near, far, zin, plus, minus, across, finish):
        def start():
            send(blocks.at[pl.ds(4, 4)], zin, (n, "z"), across)

        def whole(d, rows):
            return up(blocks[d, rows]) + up(zin[d, rows])

        def middle():
            arrived(zin, (n, "z"))
            for j, key, dev in ((0, "pf", plus), (1, "mf", minus)):
                blocks[2, halves[j]] = whole(2, halves[j]).astype(BF16)
                send(blocks.at[2, pl.ds(j * LEN, LEN)], near.at[j], (n, key), dev)

        def through(d, j, key, to, out, dev):
            arrived(near.at[j], (n, key))
            blocks[d, halves[j]] = (whole(d, halves[j]) + up(near[j])).astype(BF16)
            blocks[d, halves[1 - j]] = whole(d, halves[1 - j]).astype(BF16)
            send(blocks.at[d], far.at[to], (n, out), dev)

        def last():
            arrived(far.at[0], (n, "p2"))
            arrived(far.at[1], (n, "m2"))
            finish(whole(0, slice(0, ROWS)) + (up(far[0]) + up(far[1])))

        step(f"{n}.zm", middle)
        step(f"{n}.mp", through, 1, 0, "pf", 0, "p2", plus)
        step(f"{n}.mm", through, 3, 1, "mf", 1, "m2", minus)
        step(f"{n}.last", last)
        return start

    def proxy(s):
        first, width = GP[s]
        n, ring_first = f"p{s}", ROUTE_P[s] == "z"

        def finish(total):
            total = total.astype(BF16)
            for j in range(ROWS // LEN):
                pp[halves[j], first : first + width] = keep(j, total[halves[j]])

        if ring_first:
            start = ring_sum(
                n, ps[s], pnear[s], pfar[s], pz[s], yp, ym, zl_dev, lambda: ps[s][0], lambda: ps[s][1], finish
            )
        else:
            start = cross_sum(n, ps[s], pnear[s], pfar[s], pz[s], yp, ym, zl_dev, finish)

        def partial():
            @pl.loop(0, 2 * NY)
            def _(i):
                dy, r = (i // 2, i % 2) if ring_first else (i % 4, i // 4)
                dest = ((zl + r) % 2) * NY + (y + dy) % NY
                rows = pl.ds(pl.multiple_of(dest * CT + first, 128), width)
                ps[s][i] = dot_t(fw[...], vg[rows, :]).astype(BF16)

            start()

        step(f"{n}.part", partial)

    def gradient(s):
        first, width = GP[s]
        n, cols = f"g{s}", slice(first, first + width)

        def rows(i, c):
            return wrows(((x + i // 2) % NX) * 4 + ((zh + i % 2) % 2) * 2 + c)

        def early():
            @pl.loop(0, 2 * NX)
            def _(i):
                gpre[s][i] = dot(at[rows(i, 1 - core), :], dl[:, cols])
                gown[s][i] = dot(at[rows(i, core), :], dl[:, cols])

        def term(i, c, had):
            of_out = dot(gt[rows(i, c), :], pp[:, cols])
            if EARLY[s]:
                return had[i] + of_out
            return dot(at[rows(i, c), :], dl[:, cols]) + of_out

        def for_sibling():
            @pl.loop(0, 2 * NX)
            def _(i):
                gsib[s][i] = term(i, 1 - core, gpre[s]).astype(BF16)

            send(gsib[s], gcore[s], (n, "c"), sib)

        def for_own():
            @pl.loop(0, 2 * NX)
            def _(i):
                gown[s][i] = term(i, core, gown[s])

        def finish(total):
            res[:, cols] = total
            square = jnp.sum((total * total).reshape(WR // 8, 8, width), axis=0)
            square = sum(square[:, k : k + 128] for k in range(0, width, 128))
            sc[0] = square if s == 0 else sc[0] + square

        start = ring_sum(
            n, gs[s], gnear[s], gfar[s], gz[s], xp, xm, z_dev, lambda: gown[s][0], lambda: gown[s][1], finish
        )

        def combine():
            arrived(gcore[s], (n, "c"))

            @pl.loop(0, 2 * NX)
            def _(i):
                whole = gown[s][i] + up(gcore[s][i])
                gown[s][i] = whole
                gs[s][i] = whole.astype(BF16)

            start()

        if EARLY[s]:
            step(f"{n}.pre", early)
        step(f"{n}.sb", for_sibling)
        step(f"{n}.ow", for_own)
        step(f"{n}.comb", combine)

    for s in range(len(GP)):
        proxy(s)
        gradient(s)

    for name in ORDER:
        steps.pop(name)()
    assert not steps

    base = 0
    for devs in ((sib, xp, xm, x2, xps, xms, x2s), (zl_dev, z_dev, zd_dev), (yp, ym, y2)):
        for j, dev in enumerate(devs):
            send(sc.at[base], sc.at[base + 1 + j], ("q", base, j), dev)
        total = sc[base]
        for j in range(len(devs)):
            arrived(sc.at[base + 1 + j], ("q", base, j))
            total = total + sc[base + 1 + j]
        base = base + 1 + len(devs)
        sc[base] = total
    scale = lax.rsqrt(jnp.sum(sc[base]) / (D * PD) + 1e-6)
    out_ref[...] = (res[...] * scale).astype(BF16)
    for copy in sent:
        copy.wait_send()
    assert len(sems) <= SEMS


def per_device(activations, cotangent, lengths, grow_operator, proxy_weight):
    anywhere = pl.BlockSpec(memory_space=pl.ANY)

    def for_pieces(rows, shapes, kind=BF16):
        return [pltpu.VMEM(shape + (rows, width), kind) for (_, width), shape in zip(GP, shapes)]

    def same(*shape):
        return [shape] * len(GP)

    def routed(ring, cross):
        return [ring if route == "z" else cross for route in ROUTE_P]

    near = [
        pltpu.VMEM((2, ROWS if route == "z" else LEN, width), BF16) for (_, width), route in zip(GP, ROUTE_P)
    ]
    pre = [
        pltpu.VMEM((2 * NX, WR, width) if early else (8, 128), F32) for (_, width), early in zip(GP, EARLY)
    ]
    return pl.pallas_call(
        kernel,
        out_shape=jax.ShapeDtypeStruct((WR, CT), BF16),
        in_specs=[anywhere] * 4 + [pl.BlockSpec(memory_space=pltpu.SMEM)],
        out_specs=pl.BlockSpec(memory_space=pltpu.VMEM),
        scratch_shapes=[
            pltpu.VMEM((ROWS, D), BF16),
            pltpu.VMEM((ROWS, D), BF16),
            pltpu.VMEM((D, ROWS), BF16),
            pltpu.VMEM((D, ROWS), BF16),
            pltpu.VMEM((PD, CT), BF16),
            pltpu.VMEM((ROWS, PD), BF16),
            pltpu.VMEM((ROWS, CT), BF16),
            pltpu.VMEM((ROWS, CT), BF16),
            pltpu.VMEM((ROWS, CT), BF16),
            pltpu.VMEM((WR, CT), F32),
            pltpu.VMEM((17, 8, 128), F32),
            pltpu.SemaphoreType.DMA((3 + len(WP),)),
            pltpu.SemaphoreType.DMA((SEMS,)),
            pltpu.SemaphoreType.DMA((SEMS,)),
        ]
        + [pltpu.VMEM((D, width), BF16) for _, width in WP]
        + for_pieces(ROWS, same(2 * NY))
        + near
        + for_pieces(ROWS, routed((4,), (2,)))
        + for_pieces(ROWS, routed((), (4,)))
        + for_pieces(WR, same(2 * NX))
        + for_pieces(WR, same(2 * NX))
        + for_pieces(WR, same(2 * NX), F32)
        + for_pieces(WR, same(2 * NX))
        + for_pieces(WR, same(2))
        + for_pieces(WR, same(4))
        + for_pieces(WR, same())
        + pre,
        compiler_params=pltpu.CompilerParams(
            collective_id=0, has_side_effects=True, vmem_limit_bytes=63 * 1024 * 1024
        ),
    )(activations, cotangent, grow_operator, proxy_weight, lengths)


def solution(mesh):
    placed = (P("fsdp", None), P("fsdp", None), P("fsdp"), P("fsdp", "tp"), P("fsdp", "tp"))
    return jax.shard_map(
        per_device, mesh=mesh, in_specs=placed, out_specs=P("fsdp", "tp"), check_vma=False
    )
```

time: 504 us -> 142 us (0.28)
  waiting for transfers between devices: 360 us -> 0 us
  Pallas kernels: 0 us -> 140 us
  blocking collectives: 64.5 us -> 0 us
  matrix products: 48.2 us -> 0 us
  between operations: 13.8 us -> 0.01 us
  local copies, waits for them, and re-layouts: 13.3 us -> 1.72 us
    reduce_scatter x2 -> x0, waiting for transfers between devices: 194 us -> none  [the longest x1 111 us: per_device(): lax.psum_scatter(contract_tokens(activations, delta_cols) + contract_toke...]
    all_gather x3 -> x0, waiting for transfers between devices: 164 us -> none  [the longest x1 61 us: per_device(): lax.all_gather(grow_operator, 'fsdp', axis=0, tiled=True)]
    pallas_call x0 -> x1, Pallas kernels: none -> 140 us  [per_device(): pl.pallas_call(kernel, out_shape=jax.ShapeDtypeStruct((WR, CT), BF16), in...]
    psum x1 -> x0, blocking collectives: 64.5 us -> none  [per_device(): total = lax.psum(jnp.sum(grad_block * grad_block), ('fsdp', 'tp'))]
    dot_general x4 -> x0, matrix products: 48.2 us -> none  [the longest x2 26.9 us: contract_tokens(): lax.dot_general(left, right, (((0,), (0,)), ((), ())), preferred_element_...]
    unnamed x4 -> x1, local copies, waits for them, and re-layouts: 13.3 us -> 1.72 us
  transfers between devices with their start and end apart: 5 -> 0, of which waited for: 5 -> 0; matrix products, arithmetic and copies ran while one was open for 4% -> 0% of each run, Pallas kernels for 0% -> 0%
where the time goes in v2:
time: 142 us
  Pallas kernels  140 us (99%)
  local copies, waits for them, and re-layouts  1.72 us (1%)
    pallas_call x1, Pallas kernels, per_device(): pl.pallas_call(kernel, out_shape=jax.ShapeDtypeStruct((WR, CT), BF16), in...  140 us

profile of v2, /device:TPU:0, one launch (start us, length us, event | category | flops | bytes accessed | tf_op | source)
XLA Modules:
  0.0 142.0 jit_solution(14322843215943337637)
XLA Ops:
  0.0 140.2 %shard_map.55 = bf16[320,512]{1,0:T(8,128)(2,1)} custom-call(bf16[512,5120]{1,0:T(8,128)(2,1)} %a_hbm.1, bf16[512,5120]{1,0:T(8,128)(2,1)} %g_hbm.1, bf16[320,512]{1,0:T(8,128)(2,1)} %w_hbm.1, bf16[256,512]{1,0:T(8,128)(2,1)} %v_hbm.1, s32[2]{0:T(128)} %len_ref.1), custom_call_target="tpu_custom_call" | custom-call | tf_op jit(solution)/shard_map/pallas_call | solution.py:494
  140.3 1.7 %copy.7 = bf16[320,512]{1,0:T(8,128)(2,1)} copy(bf16[320,512]{1,0:T(8,128)(2,1)} %shard_map.55) | data formatting | bytes 655360

commit v3 on v2

--- a/solution.py
+++ b/solution.py
@@ -20,28 +20,29 @@
 
 WP = ((0, 128), (128, 128), (256, 256))
 GP = ((0, 128), (128, 128), (256, 128), (384, 128))
-ROUTE_B = "zzz"
-ROUTE_P = "zyyz"
-EARLY = (0, 1, 1, 1)
+ROUTE_B = "zzy"
+ROUTE_P = "zzzz"
+EARLY = (1, 1, 1, 1)
 SEMS = 192
 
 ORDER = (
-    "w0.start", "w1.start", "w0.a0", "w0.b0", "w0.z", "ta0", "w1.a0", "w1.b0",
-    "w1.z", "w2.start", "ta1", "ta2", "w0.a1", "w0.f0", "ta3", "w0.b1",
-    "w1.a1", "tg0", "tg1", "w1.f0", "w2.z", "v.start", "tg2", "w1.b1",
-    "w2.a0", "tg3", "w0.f1", "w0.sib", "b0.proj", "w1.f1", "w2.b0", "b0.fwd",
-    "w1.sib", "b1.proj", "w2.a1", "w2.b1", "b1.fwd", "b0.yb", "b0.z", "v.z",
-    "b1.yb", "b1.z", "v.a0", "v.b0", "b0.ya", "w2.f0", "w2.f1", "w2.sib",
-    "b1.ya", "b2.proj", "b2.fwd", "b0.end", "v.a1", "v.b1", "b1.end", "b2.z",
-    "v.f0", "v.f1", "b2.yb", "v.sib", "p0.part", "p1.part", "b2.ya", "p2.part",
-    "p0.mm", "p3.part", "p0.mp", "b2.end", "delta", "p1.zm", "p0.eo", "p3.mp",
-    "g1.pre", "p3.mm", "g2.pre", "p1.mm", "p1.mp", "g3.pre", "p2.zm", "p3.eo",
-    "p1.last", "p0.last", "g0.sb", "g0.ow", "g0.comb", "g1.sb", "g1.ow", "g0.mm",
-    "g0.mp", "p2.mm", "p2.mp", "p3.last", "g1.comb", "g0.eo", "p2.last", "g2.sb",
-    "g0.last", "g1.mm", "g1.mp", "g2.ow", "g2.comb", "g3.sb", "g1.eo", "g3.ow",
-    "g2.mm", "g2.mp", "g3.comb", "g1.last", "g2.eo", "g3.mm", "g3.mp", "g2.last",
-    "g3.eo", "g3.last",
+    "w0.start", "w1.start", "ta0", "w0.a0", "w0.b0", "w0.z", "ta1", "w1.a0",
+    "w1.b0", "w1.z", "w2.start", "ta2", "ta3", "w0.f0", "w0.a1", "tg0",
+    "w0.b1", "w1.a1", "tg1", "w1.f0", "tg2", "tg3", "w2.z", "v0.start",
+    "w1.b1", "w2.a0", "w0.f1", "w0.sib", "b0.proj", "w2.b0", "b0.fwd", "w1.f1",
+    "w2.b1", "w2.a1", "w1.sib", "b1.proj", "v0.z", "b1.fwd", "b0.yb", "b0.z",
+    "v0.b0", "v0.a0", "b1.yb", "b1.z", "w2.f0", "w2.f1", "b0.ya", "w2.sib",
+    "b2.proj", "b2.fwd", "b1.ya", "v0.b1", "v0.a1", "b0.end", "v0.f0", "b2.ya",
+    "v0.f1", "b2.yb", "b1.end", "v0.sib", "p0.part", "p0.go", "p1.part", "b2.z",
+    "p2.part", "p0.mm", "p3.part", "p0.mp", "p1.go", "p0.eo", "p1.mm", "b2.end",
+    "delta", "p1.mp", "p2.go", "pre0", "p1.eo", "p0.last", "g0.sb", "p2.mm",
+    "g0.ow", "g0.comb", "p2.mp", "p3.go", "p1.last", "g1.sb", "p2.eo", "g1.ow",
+    "g0.mm", "g0.mp", "g1.comb", "p3.mm", "pre1", "p3.mp", "p2.last", "g0.eo",
+    "g2.sb", "p3.eo", "g2.ow", "g2.comb", "g1.mm", "g0.last", "g1.mp", "p3.last",
+    "g3.sb", "g2.mm", "g3.ow", "g3.comb", "g1.eo", "g2.mp", "g2.eo", "g3.mm",
+    "g3.mp", "g1.last", "g2.last", "g3.eo", "g3.last",
 )
+VMEM_BYTES = 63 * 1024 * 1024
 
 
 def dot(a, b):
@@ -58,8 +59,8 @@
 
 def kernel(a_hbm, g_hbm, w_hbm, v_hbm, len_ref, out_ref, *scratch):
     scratch = list(scratch)
-    av, gv, at, gt, vg, bg, fw, dl, pp, res, sc, local, ss, rs = scratch[:14]
-    del scratch[:14]
+    av, gv, at, gt, vg, bg, fw, dl, pp, sc, local, ss, rs = scratch[:13]
+    del scratch[:13]
 
     def take(count):
         got = scratch[:count]
@@ -202,7 +203,7 @@
 
     for c, (first, width) in enumerate(WP):
         gather(f"w{c}", w_hbm.at[:, pl.ds(first, width)], w_place(c), load_w[c])
-    gather("v", v_hbm, lambda src: vg.at[vrows(src)], loads[2])
+    gather("v0", v_hbm, lambda src: vg.at[vrows(src)], loads[2])
 
     def keep(j, block):
         row_of = lax.broadcasted_iota(jnp.int32, block.shape, 0)
@@ -386,9 +387,8 @@
                 rows = pl.ds(pl.multiple_of(dest * CT + first, 128), width)
                 ps[s][i] = dot_t(fw[...], vg[rows, :]).astype(BF16)
 
-            start()
-
         step(f"{n}.part", partial)
+        step(f"{n}.go", start)
 
     def gradient(s):
         first, width = GP[s]
@@ -396,12 +396,6 @@
 
         def rows(i, c):
             return wrows(((x + i // 2) % NX) * 4 + ((zh + i % 2) % 2) * 2 + c)
-
-        def early():
-            @pl.loop(0, 2 * NX)
-            def _(i):
-                gpre[s][i] = dot(at[rows(i, 1 - core), :], dl[:, cols])
-                gown[s][i] = dot(at[rows(i, core), :], dl[:, cols])
 
         def term(i, c, had):
             of_out = dot(gt[rows(i, c), :], pp[:, cols])
@@ -422,7 +416,7 @@
                 gown[s][i] = term(i, core, gown[s])
 
         def finish(total):
-            res[:, cols] = total
+            gpre[s][0] = total
             square = jnp.sum((total * total).reshape(WR // 8, 8, width), axis=0)
             square = sum(square[:, k : k + 128] for k in range(0, width, 128))
             sc[0] = square if s == 0 else sc[0] + square
@@ -442,15 +436,26 @@
 
             start()
 
-        if EARLY[s]:
-            step(f"{n}.pre", early)
         step(f"{n}.sb", for_sibling)
         step(f"{n}.ow", for_own)
         step(f"{n}.comb", combine)
 
+    def delta_term(h):
+        first = GP[2 * h][0]
+
+        @pl.loop(0, 2 * NX)
+        def _(i):
+            base = ((x + i // 2) % NX) * 4 + ((zh + i % 2) % 2) * 2
+            for c, to in ((1 - core, gpre), (core, gown)):
+                both = dot(at[wrows(base + c), :], dl[:, first : first + 256])
+                to[2 * h][i] = both[:, 0:128]
+                to[2 * h + 1][i] = both[:, 128:256]
+
     for s in range(len(GP)):
         proxy(s)
         gradient(s)
+    for h in range(len(GP) // 2):
+        step(f"pre{h}", delta_term, h)
 
     for name in ORDER:
         steps.pop(name)()
@@ -467,7 +472,8 @@
         base = base + 1 + len(devs)
         sc[base] = total
     scale = lax.rsqrt(jnp.sum(sc[base]) / (D * PD) + 1e-6)
-    out_ref[...] = (res[...] * scale).astype(BF16)
+    for s, (first, width) in enumerate(GP):
+        out_ref[:, first : first + width] = (gpre[s][0] * scale).astype(BF16)
     for copy in sent:
         copy.wait_send()
     assert len(sems) <= SEMS
@@ -506,7 +512,6 @@
             pltpu.VMEM((ROWS, CT), BF16),
             pltpu.VMEM((ROWS, CT), BF16),
             pltpu.VMEM((ROWS, CT), BF16),
-            pltpu.VMEM((WR, CT), F32),
             pltpu.VMEM((17, 8, 128), F32),
             pltpu.SemaphoreType.DMA((3 + len(WP),)),
             pltpu.SemaphoreType.DMA((SEMS,)),
@@ -526,7 +531,7 @@
         + for_pieces(WR, same())
         + pre,
         compiler_params=pltpu.CompilerParams(
-            collective_id=0, has_side_effects=True, vmem_limit_bytes=63 * 1024 * 1024
+            collective_id=0, has_side_effects=True, vmem_limit_bytes=VMEM_BYTES
         ),
     )(activations, cotangent, grow_operator, proxy_weight, lengths)
 

time: 142 us -> 130 us (0.915)
  Pallas kernels: 140 us -> 128 us
    pallas_call x1, Pallas kernels: 140 us -> 128 us  [per_device(): pl.pallas_call(kernel, out_shape=jax.ShapeDtypeStruct((WR, CT), BF16), in...]
where the time goes in v3:
time: 130 us
  Pallas kernels  128 us (98%)
  local copies, waits for them, and re-layouts  1.72 us (1%)
    pallas_call x1, Pallas kernels, per_device(): pl.pallas_call(kernel, out_shape=jax.ShapeDtypeStruct((WR, CT), BF16), in...  128 us

profile of v3, /device:TPU:0, one launch (start us, length us, event | category | flops | bytes accessed | tf_op | source)
XLA Modules:
  0.0 129.6 jit_solution(14211025956199493892)
XLA Ops:
  0.0 127.8 %shard_map.55 = bf16[320,512]{1,0:T(8,128)(2,1)} custom-call(bf16[512,5120]{1,0:T(8,128)(2,1)} %a_hbm.1, bf16[512,5120]{1,0:T(8,128)(2,1)} %g_hbm.1, bf16[320,512]{1,0:T(8,128)(2,1)} %w_hbm.1, bf16[256,512]{1,0:T(8,128)(2,1)} %v_hbm.1, s32[2]{0:T(128)} %len_ref.1), custom_call_target="tpu_custom_call" | custom-call | tf_op jit(solution)/shard_map/pallas_call | solution.py:500
  127.9 1.7 %copy.7 = bf16[320,512]{1,0:T(8,128)(2,1)} copy(bf16[320,512]{1,0:T(8,128)(2,1)} %shard_map.55) | data formatting | bytes 655360

commit v4 on v3

--- a/solution.py
+++ b/solution.py
@@ -141,7 +141,7 @@
             loads[0 if src is av else 1].wait()
         part = D // 128 // 4
 
-        @pl.loop(quarter * part, (quarter + 1) * part)
+        @pl.loop(quarter * part, (quarter + 1) * part, unroll=2)
         def _(j):
             col = pl.multiple_of(j * 128, 128)
             dst[pl.ds(col, 128), :] = src[:, pl.ds(col, 128)].T
@@ -225,7 +225,7 @@
             return bg.at[pl.ds(j * LEN, LEN), cols(tid(dy, 0))]
 
         def project():
-            @pl.loop(0, ROWS // LEN)
+            @pl.loop(0, ROWS // LEN, unroll=2)
             def _(j):
                 r0 = pl.ds(pl.multiple_of(j * LEN, LEN), LEN)
                 bg[r0, cols(t)] = keep(j, dot(gv[r0, :], wg[c][...]).astype(BF16))
@@ -239,7 +239,7 @@
                 send(own, own, (n, "z", 0), zl_dev)
 
         def forward():
-            @pl.loop(0, ROWS // LEN)
+            @pl.loop(0, ROWS // LEN, unroll=2)
             def _(j):
                 r0 = pl.ds(pl.multiple_of(j * LEN, LEN), LEN)
                 fw[r0, first : first + width] = dot(av[r0, :], wg[c][...]).astype(BF16)
@@ -380,7 +380,7 @@
             start = cross_sum(n, ps[s], pnear[s], pfar[s], pz[s], yp, ym, zl_dev, finish)
 
         def partial():
-            @pl.loop(0, 2 * NY)
+            @pl.loop(0, 2 * NY, unroll=4)
             def _(i):
                 dy, r = (i // 2, i % 2) if ring_first else (i % 4, i // 4)
                 dest = ((zl + r) % 2) * NY + (y + dy) % NY
@@ -404,14 +404,14 @@
             return dot(at[rows(i, c), :], dl[:, cols]) + of_out
 
         def for_sibling():
-            @pl.loop(0, 2 * NX)
+            @pl.loop(0, 2 * NX, unroll=4)
             def _(i):
                 gsib[s][i] = term(i, 1 - core, gpre[s]).astype(BF16)
 
             send(gsib[s], gcore[s], (n, "c"), sib)
 
         def for_own():
-            @pl.loop(0, 2 * NX)
+            @pl.loop(0, 2 * NX, unroll=4)
             def _(i):
                 gown[s][i] = term(i, core, gown[s])
 
@@ -443,7 +443,7 @@
     def delta_term(h):
         first = GP[2 * h][0]
 
-        @pl.loop(0, 2 * NX)
+        @pl.loop(0, 2 * NX, unroll=2)
         def _(i):
             base = ((x + i // 2) % NX) * 4 + ((zh + i % 2) % 2) * 2
             for c, to in ((1 - core, gpre), (core, gown)):

time: 130 us -> 127 us (0.977)
  Pallas kernels: 128 us -> 125 us
    pallas_call x1, Pallas kernels: 128 us -> 125 us  [per_device(): pl.pallas_call(kernel, out_shape=jax.ShapeDtypeStruct((WR, CT), BF16), in...]
where the time goes in v4:
time: 127 us
  Pallas kernels  125 us (98%)
  local copies, waits for them, and re-layouts  1.72 us (1%)
    pallas_call x1, Pallas kernels, per_device(): pl.pallas_call(kernel, out_shape=jax.ShapeDtypeStruct((WR, CT), BF16), in...  125 us

profile of v4, /device:TPU:0, one launch (start us, length us, event | category | flops | bytes accessed | tf_op | source)
XLA Modules:
  0.0 126.7 jit_solution(11419316099417917738)
XLA Ops:
  0.0 125.0 %shard_map.55 = bf16[320,512]{1,0:T(8,128)(2,1)} custom-call(bf16[512,5120]{1,0:T(8,128)(2,1)} %a_hbm.1, bf16[512,5120]{1,0:T(8,128)(2,1)} %g_hbm.1, bf16[320,512]{1,0:T(8,128)(2,1)} %w_hbm.1, bf16[256,512]{1,0:T(8,128)(2,1)} %v_hbm.1, s32[2]{0:T(128)} %len_ref.1), custom_call_target="tpu_custom_call" | custom-call | tf_op jit(solution)/shard_map/pallas_call | solution.py:500
  125.0 1.7 %copy.7 = bf16[320,512]{1,0:T(8,128)(2,1)} copy(bf16[320,512]{1,0:T(8,128)(2,1)} %shard_map.55) | data formatting | bytes 655360

commit v5 on v4

--- a/solution.py
+++ b/solution.py
@@ -21,26 +21,26 @@
 WP = ((0, 128), (128, 128), (256, 256))
 GP = ((0, 128), (128, 128), (256, 128), (384, 128))
 ROUTE_B = "zzy"
-ROUTE_P = "zzzz"
+ROUTE_P = "zzzy"
 EARLY = (1, 1, 1, 1)
 SEMS = 192
 
 ORDER = (
-    "w0.start", "w1.start", "ta0", "w0.a0", "w0.b0", "w0.z", "ta1", "w1.a0",
-    "w1.b0", "w1.z", "w2.start", "ta2", "ta3", "w0.f0", "w0.a1", "tg0",
-    "w0.b1", "w1.a1", "tg1", "w1.f0", "tg2", "tg3", "w2.z", "v0.start",
-    "w1.b1", "w2.a0", "w0.f1", "w0.sib", "b0.proj", "w2.b0", "b0.fwd", "w1.f1",
-    "w2.b1", "w2.a1", "w1.sib", "b1.proj", "v0.z", "b1.fwd", "b0.yb", "b0.z",
-    "v0.b0", "v0.a0", "b1.yb", "b1.z", "w2.f0", "w2.f1", "b0.ya", "w2.sib",
-    "b2.proj", "b2.fwd", "b1.ya", "v0.b1", "v0.a1", "b0.end", "v0.f0", "b2.ya",
-    "v0.f1", "b2.yb", "b1.end", "v0.sib", "p0.part", "p0.go", "p1.part", "b2.z",
-    "p2.part", "p0.mm", "p3.part", "p0.mp", "p1.go", "p0.eo", "p1.mm", "b2.end",
-    "delta", "p1.mp", "p2.go", "pre0", "p1.eo", "p0.last", "g0.sb", "p2.mm",
-    "g0.ow", "g0.comb", "p2.mp", "p3.go", "p1.last", "g1.sb", "p2.eo", "g1.ow",
-    "g0.mm", "g0.mp", "g1.comb", "p3.mm", "pre1", "p3.mp", "p2.last", "g0.eo",
-    "g2.sb", "p3.eo", "g2.ow", "g2.comb", "g1.mm", "g0.last", "g1.mp", "p3.last",
-    "g3.sb", "g2.mm", "g3.ow", "g3.comb", "g1.eo", "g2.mp", "g2.eo", "g3.mm",
-    "g3.mp", "g1.last", "g2.last", "g3.eo", "g3.last",
+    "w0.start", "w2.start", "w0.z", "w1.start", "w2.z", "w0.b0", "ta0", "w2.b0",
+    "w0.b1", "w1.z", "ta1", "ta2", "ta3", "w2.a0", "w0.a1", "tg0",
+    "tg1", "w0.a0", "w2.a1", "tg2", "w2.b1", "w1.b0", "w1.a1", "w1.a0",
+    "w0.f0", "v0.start", "w0.f1", "w0.sib", "w2.f0", "b0.proj", "w2.f1", "w2.sib",
+    "b2.proj", "tg3", "w1.b1", "v0.z", "b0.fwd", "b0.z", "w1.f0", "w1.f1",
+    "v0.a0", "w1.sib", "b1.proj", "b2.ya", "v0.b0", "b2.yb", "v0.b1", "v0.a1",
+    "b1.z", "b0.yb", "b2.fwd", "b1.fwd", "b1.yb", "b2.z", "b0.ya", "v0.f0",
+    "v0.f1", "v0.sib", "b1.ya", "p0.part", "p0.go", "b0.end", "p1.part", "p3.part",
+    "p3.go", "p0.mm", "p0.mp", "p1.go", "b2.end", "b1.end", "delta", "p2.part",
+    "pre0", "p1.mm", "p0.eo", "p1.mp", "p2.go", "pre1", "p1.eo", "p0.last",
+    "g0.sb", "p2.mm", "p2.mp", "g0.ow", "g0.comb", "p3.zm", "p1.last", "g1.sb",
+    "p2.eo", "g1.ow", "g1.comb", "p3.mp", "g0.mm", "p3.mm", "g0.mp", "p2.last",
+    "g2.sb", "g1.mm", "g2.ow", "p3.last", "g2.comb", "g3.sb", "g3.ow", "g3.comb",
+    "g0.eo", "g1.mp", "g2.mm", "g2.mp", "g3.mm", "g1.eo", "g2.eo", "g3.mp",
+    "g3.eo", "g0.last", "g1.last", "g2.last", "g3.last",
 )
 VMEM_BYTES = 63 * 1024 * 1024
 

time: 127 us -> 125 us (0.984)
  Pallas kernels: 125 us -> 123 us
    pallas_call x1, Pallas kernels: 125 us -> 123 us  [per_device(): pl.pallas_call(kernel, out_shape=jax.ShapeDtypeStruct((WR, CT), BF16), in...]
where the time goes in v5:
time: 125 us
  Pallas kernels  123 us (98%)
  local copies, waits for them, and re-layouts  1.72 us (1%)
    pallas_call x1, Pallas kernels, per_device(): pl.pallas_call(kernel, out_shape=jax.ShapeDtypeStruct((WR, CT), BF16), in...  123 us

profile of v5, /device:TPU:0, one launch (start us, length us, event | category | flops | bytes accessed | tf_op | source)
XLA Modules:
  0.0 124.6 jit_solution(15040537838903107658)
XLA Ops:
  0.0 122.9 %shard_map.55 = bf16[320,512]{1,0:T(8,128)(2,1)} custom-call(bf16[512,5120]{1,0:T(8,128)(2,1)} %a_hbm.1, bf16[512,5120]{1,0:T(8,128)(2,1)} %g_hbm.1, bf16[320,512]{1,0:T(8,128)(2,1)} %w_hbm.1, bf16[256,512]{1,0:T(8,128)(2,1)} %v_hbm.1, s32[2]{0:T(128)} %len_ref.1), custom_call_target="tpu_custom_call" | custom-call | tf_op jit(solution)/shard_map/pallas_call | solution.py:500
  122.9 1.7 %copy.7 = bf16[320,512]{1,0:T(8,128)(2,1)} copy(bf16[320,512]{1,0:T(8,128)(2,1)} %shard_map.55) | data formatting | bytes 655360

commit v6 on v5

--- a/solution.py
+++ b/solution.py
@@ -42,6 +42,7 @@
     "g0.eo", "g1.mp", "g2.mm", "g2.mp", "g3.mm", "g1.eo", "g2.eo", "g3.mp",
     "g3.eo", "g0.last", "g1.last", "g2.last", "g3.last",
 )
+LOAD_AT = "w0.z"
 VMEM_BYTES = 63 * 1024 * 1024
 
 
@@ -109,8 +110,6 @@
         pltpu.make_async_copy(w_hbm.at[:, pl.ds(first, width)], wg[c].at[wrows(f)], local.at[3 + c])
         for c, (first, width) in enumerate(WP)
     ]
-    for load in loads + load_w:
-        load.start()
 
     barrier = pltpu.get_barrier_semaphore()
     for peer in peers:
@@ -458,6 +457,9 @@
         step(f"pre{h}", delta_term, h)
 
     for name in ORDER:
+        if name == LOAD_AT:
+            for load in loads + load_w:
+                load.start()
         steps.pop(name)()
     assert not steps
 

time: 125 us -> 125 us (level)
  no operation moved by 1% of the time
where the time goes in v6:
time: 125 us
  Pallas kernels  123 us (98%)
  local copies, waits for them, and re-layouts  1.72 us (1%)
    pallas_call x1, Pallas kernels, per_device(): pl.pallas_call(kernel, out_shape=jax.ShapeDtypeStruct((WR, CT), BF16), in...  123 us

profile of v6, /device:TPU:0, one launch (start us, length us, event | category | flops | bytes accessed | tf_op | source)
XLA Modules:
  0.0 124.7 jit_solution(8521964337355384124)
XLA Ops:
  0.0 122.9 %shard_map.55 = bf16[320,512]{1,0:T(8,128)(2,1)} custom-call(bf16[512,5120]{1,0:T(8,128)(2,1)} %a_hbm.1, bf16[512,5120]{1,0:T(8,128)(2,1)} %g_hbm.1, bf16[320,512]{1,0:T(8,128)(2,1)} %w_hbm.1, bf16[256,512]{1,0:T(8,128)(2,1)} %v_hbm.1, s32[2]{0:T(128)} %len_ref.1), custom_call_target="tpu_custom_call" | custom-call | tf_op jit(solution)/shard_map/pallas_call | solution.py:502
  122.9 1.7 %copy.7 = bf16[320,512]{1,0:T(8,128)(2,1)} copy(bf16[320,512]{1,0:T(8,128)(2,1)} %shard_map.55) | data formatting | bytes 655360
